TPU v7x, 256 devices: a whole 4x4x8 slice. The times are simulated.
256 devices in a mesh: pipe: 16 (over y_lo, x, core), expert: 16 (over y_hi, z).
Axes of the slice: x: 4, y: 4 (y_hi: 2, y_lo: 2; y = y_hi * 2 + y_lo), z: 8, core: 2. Of those that a mesh axis runs over, the one named last changes fastest.
Arguments:
- held_fwd: bfloat16 [16, 1024, 3584], P('pipe', 'expert'), may hold values from -6 to 6
- ids_fwd: int32 [16, 1024], P('pipe'), may hold values from 0 to 3, as said below
- probs_fwd: bfloat16 [16, 1024], P('pipe'), may hold values from 0.19921875 to 1
- saved_in: bfloat16 [16, 1024, 3584], P('pipe', 'expert'), may hold values from -6 to 6
- held_grad: bfloat16 [16, 1024, 3584], P('pipe', 'expert'), may hold values from -6 to 6
- ids_bwd: int32 [16, 1024], P('pipe'), may hold values from 0 to 3, as said below
- probs_bwd: bfloat16 [16, 1024], P('pipe'), may hold values from 0.19921875 to 1
- w_gate: bfloat16 [16, 3584, 6144], P('pipe', None, 'expert'), may hold values from -0.09375 to 0.09375
- w_up: bfloat16 [16, 3584, 6144], P('pipe', None, 'expert'), may hold values from -0.09375 to 0.09375
- w_down: bfloat16 [16, 6144, 3584], P('pipe', 'expert'), may hold values from -0.15625 to 0.15625
Outputs:
- fwd_out: bfloat16 [16, 1024, 3584], P('pipe', 'expert')
- grad_out: bfloat16 [16, 1024, 3584], P('pipe', 'expert')
Inputs may be any that keep to these rules, and one draw needn't show every extreme that they name: `ids_fwd`: in every section one expert takes exactly 20 of the 64 rows of each device, 320 rows in all; no expert takes more than 20 of the rows of one device. `ids_bwd`: in every section one expert takes exactly 20 of the 64 rows of each device, 320 rows in all; no expert takes more than 20 of the rows of one device.
All inputs are finite; a program needn't handle non-finite values.
Results may differ from a plain program's by a relative error of at most 0.004.
Values may be sent and summed in bfloat16 or wider, within the bound.
A program may use at most 128 MiB of HBM per device.

v0:
```python
import jax
import jax.numpy as jnp
from jax import lax
from jax.sharding import PartitionSpec as P

EXPERTS = 4
SLOT = 20


def passed_along(value, axis, by):
    devices = lax.axis_size(axis)
    return lax.ppermute(value, axis, [(i, (i + by) % devices) for i in range(devices)])


def chosen_rows(routing, expert, capacity):
    matches = routing == expert
    places = jnp.nonzero(matches, size=capacity, fill_value=0)[0].astype(jnp.int32)
    filled = jnp.arange(capacity, dtype=jnp.int32) < jnp.sum(matches.astype(jnp.int32))
    return (places, filled)


def expert_forward(row_block, row_scale, gate_cols, up_cols, down_rows):
    gate_pre = jnp.dot(row_block, gate_cols, preferred_element_type=jnp.float32)
    upward = jnp.dot(row_block, up_cols, preferred_element_type=jnp.float32)
    hidden = (gate_pre * jax.nn.sigmoid(gate_pre) * upward).astype(jnp.bfloat16)
    return jnp.dot(hidden, down_rows, preferred_element_type=jnp.float32) * row_scale[:, None]


def expert_backward(row_block, grad_block, row_scale, gate_cols, up_cols, down_rows):
    gate_pre = jnp.dot(row_block, gate_cols, preferred_element_type=jnp.float32)
    upward = jnp.dot(row_block, up_cols, preferred_element_type=jnp.float32)
    d_hidden = (
        jnp.dot(grad_block, down_rows.T, preferred_element_type=jnp.float32) * row_scale[:, None]
    )
    sigmoid_gate = jax.nn.sigmoid(gate_pre)
    d_gate = (d_hidden * upward * sigmoid_gate * (1.0 + gate_pre * (1.0 - sigmoid_gate))).astype(
        jnp.bfloat16
    )
    d_up = (d_hidden * gate_pre * sigmoid_gate).astype(jnp.bfloat16)
    result = jnp.dot(d_gate, gate_cols.T, preferred_element_type=jnp.float32)
    return result + jnp.dot(d_up, up_cols.T, preferred_element_type=jnp.float32)


def expert_slots(local_ids, local_probs, slot_total):
    place_list = []
    scale_list = []
    for expert in range(EXPERTS):
        places, filled = chosen_rows(local_ids, expert, slot_total)
        place_list.append(places)
        scale_list.append(jnp.where(filled, local_probs[places], jnp.zeros((), local_probs.dtype)))
    return (jnp.stack(place_list), jnp.stack(scale_list))


def source_places(routing_all, expert, slot_total, local_total):
    blocks = routing_all.reshape(-1, local_total)

    def one_block(block_ids):
        return chosen_rows(block_ids, expert, slot_total)

    places, filled = jax.vmap(one_block)(blocks)
    offsets = (jnp.arange(blocks.shape[0], dtype=jnp.int32) * local_total)[:, None]
    return ((places + offsets).reshape(-1), filled.reshape(-1))


def combine_slots(returned, places_all, local_total):
    feature_width = returned.shape[2]
    grouped = jnp.sum(
        returned.reshape(EXPERTS, -1, returned.shape[1], feature_width), axis=1, dtype=jnp.float32
    )
    empty_rows = jnp.zeros((local_total, feature_width), jnp.float32)
    return empty_rows.at[places_all.reshape(-1)].add(grouped.reshape(-1, feature_width))


def on_device(
    held_fwd, ids_fwd, probs_fwd, saved_in, held_grad, ids_bwd, probs_bwd, w_gate, w_up, w_down
):
    devices = lax.axis_size("expert")
    group_size = devices // EXPERTS
    position = lax.axis_index("expert")
    my_expert = position // group_size
    gate_cols = w_gate[0]
    up_cols = w_up[0]
    down_rows = w_down[0]
    rows_fwd = passed_along(held_fwd[0], "pipe", 1)
    grads_in = passed_along(held_grad[0], "pipe", -1)
    saved_rows = saved_in[0]
    local_total = rows_fwd.shape[0]
    feature_width = rows_fwd.shape[1]
    slot_total = SLOT
    first_row = position * local_total
    local_fwd = lax.dynamic_slice_in_dim(ids_fwd[0], first_row, local_total)
    prob_fwd = lax.dynamic_slice_in_dim(probs_fwd[0], first_row, local_total)
    places_all, scales_all = expert_slots(local_fwd, prob_fwd, slot_total)
    local_bwd = lax.dynamic_slice_in_dim(ids_bwd[0], first_row, local_total)
    prob_bwd = lax.dynamic_slice_in_dim(probs_bwd[0], first_row, local_total)
    places_back, scales_back = expert_slots(local_bwd, prob_bwd, slot_total)
    gathered = lax.all_gather(rows_fwd, "expert", axis=0, tiled=True)
    picked, filled = source_places(ids_fwd[0], my_expert, slot_total, local_total)
    row_scale = jnp.where(filled, probs_fwd[0][picked].astype(jnp.float32), 0.0)
    partial_value = expert_forward(gathered[picked], row_scale, gate_cols, up_cols, down_rows)
    back_rows = partial_value.astype(jnp.bfloat16).reshape(devices, slot_total, feature_width)
    returned = lax.all_to_all(back_rows, "expert", split_axis=0, concat_axis=0, tiled=True)
    summed = combine_slots(returned, places_all, local_total)
    saved_all, grads_all = (
        lax.all_gather(saved_rows, "expert", axis=0, tiled=True),
        lax.all_gather(grads_in, "expert", axis=0, tiled=True),
    )
    picked_back, filled_back = source_places(ids_bwd[0], my_expert, slot_total, local_total)
    scale_back = jnp.where(filled_back, probs_bwd[0][picked_back].astype(jnp.float32), 0.0)
    partial_back = expert_backward(
        saved_all[picked_back], grads_all[picked_back], scale_back, gate_cols, up_cols, down_rows
    )
    back_grads = partial_back.astype(jnp.bfloat16).reshape(devices, slot_total, feature_width)
    returned_back = lax.all_to_all(back_grads, "expert", split_axis=0, concat_axis=0, tiled=True)
    summed_back = combine_slots(returned_back, places_back, local_total)
    fwd_rows = (rows_fwd + summed).astype(jnp.bfloat16)
    grad_rows = (grads_in + summed_back).astype(jnp.bfloat16)
    return (fwd_rows[None], grad_rows[None])


def solution(mesh):
    return jax.shard_map(
        on_device,
        mesh=mesh,
        in_specs=(
            P("pipe", "expert", None),
            P("pipe", None),
            P("pipe", None),
            P("pipe", "expert", None),
            P("pipe", "expert", None),
            P("pipe", None),
            P("pipe", None),
            P("pipe", None, "expert"),
            P("pipe", None, "expert"),
            P("pipe", "expert", None),
        ),
        out_specs=(P("pipe", "expert", None), P("pipe", "expert", None)),
        check_vma=False,
    )
```

profile of v0, /device:TPU:4, one launch (start us, length us, event | category | flops | bytes accessed | tf_op | source)
XLA Modules:
  0.0 528.6 jit_solution(459751190031298476)
XLA Ops:
  7.2 0.7 all-gather.9.cloned.1.call-update
  8.1 6.3 %collective-permute-done.1 = bf16[64,3584]{1,0:T(8,128)(2,1)S(1)} collective-permute-done((bf16[64,3584]{1,0:T(8,128)(2,1)}, bf16[64,3584]{1,0:T(8,128)(2,1)S(1)}, u32[]{:S(2)}, u32[]{:S(2)}) %collective-permute-start.1) | collective-permute-done | bytes 458784 | tf_op jit(solution)/shard_map/ppermute | solution.py:12
  14.4 0.8 copy-done.2
  15.2 1.7 collective-permute-start
  16.9 6.5 %collective-permute-done = bf16[64,3584]{1,0:T(8,128)(2,1)S(1)} collective-permute-done((bf16[64,3584]{1,0:T(8,128)(2,1)}, bf16[64,3584]{1,0:T(8,128)(2,1)S(1)}, u32[]{:S(2)}, u32[]{:S(2)}) %collective-permute-start) | collective-permute-done | bytes 458784 | tf_op jit(solution)/shard_map/ppermute | solution.py:12
  23.5 0.8 copy-done.4
  24.3 0.6 broadcast.1193
  24.9 1.4 fusion.108
  26.3 0.3 copy.52
  26.6 0.9 compare_select_fusion.1
  27.5 1.3 copy.53
  28.9 0.3 copy.61
  29.2 0.9 compare_select_fusion
  30.1 1.3 copy.62
  31.9 7.4 %scatter_custom_fusion.10 = s32[320]{0:T(512)S(1)} fusion(s32[1024]{0:T(1024)S(1)} %reshape.1353, s32[1024]{0:T(1024)S(1)} %broadcast.1072, s32[]{:T(128)} %constant.206.clone.1), kind=kCustom, calls=%fused_computation.151 | custom fusion | flops 1024 | bytes 1284
  40.0 8.1 %scatter_custom_fusion.11 = s32[320]{0:T(512)S(1)} fusion(s32[1024]{0:T(1024)S(1)} %reshape.1359, s32[1024]{0:T(1024)S(1)} %broadcast.1072, s32[]{:T(128)} %constant.206.clone.1), kind=kCustom, calls=%fused_computation.149 | custom fusion | flops 1024 | bytes 1284
  49.6 2.5 gather_fusion.3
  52.0 87.1 %all-gather.9.cloned.1.call-done = bf16[1,1024,3584]{2,1,0:T(8,128)(2,1)} async-done(((bf16[1,64,3584]{2,1,0:T(8,128)(2,1)}), bf16[1,1024,3584]{2,1,0:T(8,128)(2,1)}) %all-gather.9.cloned.1.call-update) | async-done | bytes 7340048 | tf_op jit(solution)/shard_map/all_gather | solution.py:105
  139.1 11.5 %gather_fusion.4 = bf16[320,3584]{1,0:T(8,128)(2,1)} fusion(bf16[1024,3584]{1,0:T(8,128)(2,1)} %bitcast.85, s32[1024]{0:T(1024)S(1)} %pad_clamp_fusion), kind=kCustom, calls=%fused_computation.4 | custom fusion | bytes 4588800 | tf_op jit(solution)/shard_map/gather | solution.py:111
  150.6 4.1 fusion.12
  154.6 110.0 %all-gather.7.cloned.1.call-done = bf16[1024,3584]{1,0:T(8,128)(2,1)} async-done(((bf16[64,3584]{1,0:T(8,128)(2,1)}), bf16[1024,3584]{1,0:T(8,128)(2,1)}) %all-gather.7.cloned.1.call-update) | async-done | bytes 7340048 | tf_op jit(solution)/shard_map/all_gather | solution.py:106
  264.7 11.6 %gather_fusion.2 = bf16[320,3584]{1,0:T(8,128)(2,1)} fusion(bf16[1024,3584]{1,0:T(8,128)(2,1)} %all-gather.7.cloned.1.call-done, s32[1024]{0:T(1024)S(1)} %pad_clamp_fusion), kind=kCustom, calls=%fused_computation.2 | custom fusion | bytes 4588800 | tf_op jit(solution)/shard_map/gather | solution.py:111
  276.3 4.9 fusion.25
  281.2 7.5 %fusion.10 = f32[320,3584]{1,0:T(8,128)} fusion(bf16[1,3584,384]{2,1,0:T(8,128)(2,1)} %param.17, f32[320,384]{1,0:T(8,128)} %fusion.25, bf16[320,3584]{1,0:T(8,128)(2,1)} %gather_fusion.4, bf16[1,3584,384]{2,1,0:T(8,128)(2,1)S(1)} %copy-done, f32[320,384]{1,0:T(8,128)S(1)} %fusion.12), kind=kOutput, calls=%fused_computation.31 | convolution fusion | flops 1762836480 | bytes 13369344 | tf_op jit(solution)/shard_map/dot_general | solution.py:40
  288.7 5.3 fusion.1
  293.9 4.1 reshape.1209
  298.1 4.6 all-to-all-start.1
  302.8 2.5 gather_fusion.1
  305.3 0.7 fusion.81
  306.0 111.3 %all-gather.5.cloned.1.call-done = bf16[1024,3584]{1,0:T(8,128)(2,1)} async-done(((bf16[64,3584]{1,0:T(8,128)(2,1)}), bf16[1024,3584]{1,0:T(8,128)(2,1)}) %all-gather.5.cloned.1.call-update) | async-done | bytes 7340048 | tf_op jit(solution)/shard_map/all_gather | solution.py:97
  417.4 11.5 %gather_fusion = bf16[320,3584]{1,0:T(8,128)(2,1)} fusion(bf16[1024,3584]{1,0:T(8,128)(2,1)} %all-gather.5.cloned.1.call-done, s32[1024]{0:T(1024)S(1)} %pad_clamp_fusion.1), kind=kCustom, calls=%fused_computation | custom fusion | bytes 4588800 | tf_op jit(solution)/shard_map/gather | solution.py:100
  428.9 3.0 fusion.8
  431.8 5.9 %fusion = bf16[320,3584]{1,0:T(8,128)(2,1)S(1)} fusion(bf16[1,384,3584]{2,1,0:T(8,128)(2,1)} %param.19, f32[320]{0:T(512)S(1)} %convert_select_fusion.1, f32[320,384]{1,0:T(8,128)S(1)} %fusion.8, bf16[320,3584]{1,0:T(8,128)(2,1)} %gather_fusion, bf16[1,3584,384]{2,1,0:T(8,128)(2,1)} %param.17), kind=kOutput, calls=%fused_computation.21 | convolution fusion | flops 1764638720 | bytes 10585344 | tf_op jit(solution)/shard_map/dot_general | solution.py:26
  437.8 2.2 reshape.1202
  440.0 5.7 %all-to-all-start = ((bf16[16,20,3584]{2,1,0:T(8,128)(2,1)}), bf16[16,20,3584]{2,1,0:T(8,128)(2,1)}, u32[]{:S(2)}, u32[]{:S(2)}) async-start(bf16[16,20,3584]{2,1,0:T(8,128)(2,1)} %reshape.1202), calls=%async_computation | async-start | bytes 5505024 | tf_op jit(solution)/shard_map/all_to_all | solution.py:102
  446.0 1.0 scatter_custom_fusion.7
  447.5 1.0 scatter_custom_fusion.8
  448.5 0.2 select_n.484
  449.0 1.0 scatter_custom_fusion.6
  450.0 0.2 select_n.476
  450.5 1.0 scatter_custom_fusion.5
  451.5 0.2 select_n.472
  451.7 0.7 fusion.82
  452.4 1.3 compare_select_fusion.34
  453.8 1.2 compare_select_fusion.36
  455.0 0.7 fusion.73
  456.1 1.0 scatter_custom_fusion.2
  457.1 0.2 select_n.457
  457.6 1.0 scatter_custom_fusion.3
  459.1 1.0 scatter_custom_fusion.1
  460.6 1.0 scatter_custom_fusion
  461.8 0.7 fusion.74
  462.5 1.3 compare_select_fusion.38
  463.8 1.2 compare_select_fusion.40
  465.2 1.0 convert_element_type.235
  466.2 2.4 convert_reduce_fusion
  468.6 1.2 reshape.1349
  469.7 3.1 scatter_fusion.1
  472.9 0.8 convert_bitcast_fusion
  473.7 37.6 %all-to-all-done = bf16[16,20,3584]{2,1,0:T(8,128)(2,1)} async-done(((bf16[16,20,3584]{2,1,0:T(8,128)(2,1)}), bf16[16,20,3584]{2,1,0:T(8,128)(2,1)}, u32[]{:S(2)}, u32[]{:S(2)}) %all-to-all-start) | async-done | bytes 2293792 | tf_op jit(solution)/shard_map/all_to_all | solution.py:102
  511.3 2.4 convert_reduce_fusion.1
  513.7 1.1 reshape.1309
  514.8 5.0 scatter_fusion
  519.8 2.0 convert_bitcast_fusion.1
  (105 shorter events, 6.6 us)
Async XLA Ops:
  7.2 274.0 %copy-start = (bf16[1,3584,384]{2,1,0:T(8,128)(2,1)S(1)}, bf16[1,3584,384]{2,1,0:T(8,128)(2,1)}, u32[]{:S(2)}) copy-start(bf16[1,3584,384]{2,1,0:T(8,128)(2,1)} %param.18) | copy-start | bytes 8257540
  7.2 24.2 %copy-start.9 = (s32[2]{0:T(128)S(1)}, s32[2]{0:T(128)}, u32[]{:S(2)}) copy-start(s32[2]{0:T(128)} %constant.228) | copy-start | bytes 28
  7.2 131.9 %all-gather.9.cloned.1.call-start = ((), (), s32[]{:S(2)}) async-start(), calls=%async_computation.4 | async-start | bytes 7798784 | tf_op jit(solution)/shard_map/all_gather | solution.py:105
  7.9 23.6 %copy-start.8 = (s32[2]{0:T(128)S(1)}, s32[2]{0:T(128)}, u32[]{:S(2)}) copy-start(s32[2]{0:T(128)} %constant.231) | copy-start | bytes 28
  7.9 256.7 %all-gather.7.cloned.1.call-start = ((), (), s32[]{:S(2)}) async-start(), calls=%async_computation.3 | async-start | bytes 7798784 | tf_op jit(solution)/shard_map/all_gather | solution.py:106
  8.0 6.4 %collective-permute-start.1 = (bf16[64,3584]{1,0:T(8,128)(2,1)}, bf16[64,3584]{1,0:T(8,128)(2,1)S(1)}, u32[]{:S(2)}, u32[]{:S(2)}) collective-permute-start(bf16[64,3584]{1,0:T(8,128)(2,1)} %bitcast.88), channel_id=1, source_target_pairs={{0,240},{16,0},{32,16},{48,32},{64,48},{80,64},{96,80},{112,96},{1... | collective-permute-start | bytes 1376264 | tf_op jit(solution)/shard_map/ppermute | solution.py:12
  14.4 0.8 copy-start.2
  15.2 34.3 %copy-start.6 = (bf16[1,1024]{1,0:T(2,128)(2,1)S(1)}, bf16[1,1024]{1,0:T(2,128)(2,1)}, u32[]{:S(2)}) copy-start(bf16[1,1024]{1,0:T(2,128)(2,1)} %param.16) | copy-start | bytes 6148
  15.2 402.2 %all-gather.5.cloned.1.call-start = ((), (), s32[]{:S(2)}) async-start(), calls=%async_computation.2 | async-start | bytes 7798784 | tf_op jit(solution)/shard_map/all_gather | solution.py:97
  15.2 8.3 %collective-permute-start = (bf16[64,3584]{1,0:T(8,128)(2,1)}, bf16[64,3584]{1,0:T(8,128)(2,1)S(1)}, u32[]{:S(2)}, u32[]{:S(2)}) collective-permute-start(bf16[64,3584]{1,0:T(8,128)(2,1)} %bitcast.89), channel_id=1, source_target_pairs={{0,16},{16,32},{32,48},{48,64},{64,80},{80,96},{96,112},{112,128},... | collective-permute-start | bytes 1376264 | tf_op jit(solution)/shard_map/ppermute | solution.py:12
  23.5 0.8 copy-start.4
  298.1 4.6 copy-start.7
  298.1 142.0 %all-to-all-start.1 = ((bf16[16,20,3584]{2,1,0:T(8,128)(2,1)}), bf16[16,20,3584]{2,1,0:T(8,128)(2,1)}, u32[]{:S(2)}, u32[]{:S(2)}) async-start(bf16[16,20,3584]{2,1,0:T(8,128)(2,1)} %reshape.1209), calls=%async_computation.1 | async-start | bytes 5505024 | tf_op jit(solution)/shard_map/all_to_all | solution.py:114
  440.0 25.1 %copy-start.3 = (bf16[64,3584]{1,0:T(8,128)(2,1)S(1)}, bf16[64,3584]{1,0:T(8,128)(2,1)}, u32[]{:S(2)}) copy-start(bf16[64,3584]{1,0:T(8,128)(2,1)} %copy-done.2) | copy-start | bytes 1376260
  440.0 25.1 %copy-start.5 = (bf16[64,3584]{1,0:T(8,128)(2,1)S(1)}, bf16[64,3584]{1,0:T(8,128)(2,1)}, u32[]{:S(2)}) copy-start(bf16[64,3584]{1,0:T(8,128)(2,1)} %copy-done.4) | copy-start | bytes 1376260
  440.0 71.3 %all-to-all-start = ((bf16[16,20,3584]{2,1,0:T(8,128)(2,1)}), bf16[16,20,3584]{2,1,0:T(8,128)(2,1)}, u32[]{:S(2)}, u32[]{:S(2)}) async-start(bf16[16,20,3584]{2,1,0:T(8,128)(2,1)} %reshape.1202), calls=%async_computation | async-start | bytes 5505024 | tf_op jit(solution)/shard_map/all_to_all | solution.py:102
  514.8 7.0 %copy-start.1 = (bf16[1,3584,384]{2,1,0:T(8,128)(2,1)S(1)}, bf16[1,3584,384]{2,1,0:T(8,128)(2,1)}, u32[]{:S(2)}) copy-start(bf16[1,3584,384]{2,1,0:T(8,128)(2,1)} %param.18) | copy-start | bytes 8257540
Sparse Core Ops, SparseCore 0:
  10.6 128.4 all-gather.8
  142.3 122.3 all-gather.6
  267.8 149.5 all-gather.4
where the time goes:
time: 534 us; the launch traced here: 529 us
  waiting for transfers between devices  360 us (67%)
  local copies, waits for them, and re-layouts  56.2 us (11%)
  other arithmetic  55.6 us (10%)
  matrix products  30.6 us (6%)
  between operations  14.4 us (3%)
  starting transfers between devices  12.2 us (2%)
    all_gather x1, waiting for transfers between devices, on_device(): gathered = lax.all_gather(rows_fwd, 'expert', axis=0, tiled=True)  111 us
    all_gather x1, waiting for transfers between devices, on_device(): lax.all_gather(grads_in, 'expert', axis=0, tiled=True)  110 us
    all_gather x1, waiting for transfers between devices, on_device(): lax.all_gather(saved_rows, 'expert', axis=0, tiled=True)  87.1 us
    all_to_all x1, waiting for transfers between devices, on_device(): lax.all_to_all(back_rows, 'expert', split_axis=0, concat_axis=0, tiled=True)  37.6 us
    unnamed x8, other arithmetic  15.7 us
    ppermute x2, waiting for transfers between devices, passed_along(): lax.ppermute(value, axis, [(i, (i + by) % devices) for i in range(devices)])  12.8 us
    gather x1, local copies, waits for them, and re-layouts, on_device(): grads_all[picked_back]  11.6 us
    gather x1, local copies, waits for them, and re-layouts, on_device(): gathered[picked]  11.5 us
  transfers between devices with their start and end apart: 7, of which 6 were waited for; matrix products, arithmetic and copies ran while one was open for 25% of the time, Pallas kernels for 0%

commit v1 on v0

--- a/solution.py
+++ b/solution.py
@@ -102,7 +102,10 @@
     returned = lax.all_to_all(back_rows, "expert", split_axis=0, concat_axis=0, tiled=True)
     summed = combine_slots(returned, places_all, local_total)
     saved_all, grads_all = (
-        lax.all_gather(saved_rows, "expert", axis=0, tiled=True),
+        jnp.concatenate(
+            lax.all_to_all(jnp.stack([saved_rows] * lax.axis_size("expert")), "expert", 0, 0),
+            axis=0,
+        ),
         lax.all_gather(grads_in, "expert", axis=0, tiled=True),
     )
     picked_back, filled_back = source_places(ids_bwd[0], my_expert, slot_total, local_total)

time: 534 us -> 541 us (1.013)
  waiting for transfers between devices: 360 us -> 341 us
  starting transfers between devices: 12.2 us -> 22.4 us
  local copies, waits for them, and re-layouts: 56.2 us -> 65.5 us
    all_to_all x0 -> x1, waiting for transfers between devices: none -> 155 us  [on_device(): lax.all_to_all(jnp.stack([saved_rows] * lax.axis_size('expert')), 'expert...]
    all_gather x1 -> x0, waiting for transfers between devices: 87.1 us -> none  [on_device(): lax.all_gather(saved_rows, 'expert', axis=0, tiled=True)]
    all_gather x1, waiting for transfers between devices: 110 us -> 28.4 us  [on_device(): lax.all_gather(grads_in, 'expert', axis=0, tiled=True)]
    all_to_all x0 -> x1, starting transfers between devices: none -> 11.4 us  [on_device(): lax.all_to_all(jnp.stack([saved_rows] * lax.axis_size('expert')), 'expert...]
    all_to_all x1, waiting for transfers between devices: 37.6 us -> 31.3 us  [on_device(): lax.all_to_all(back_rows, 'expert', split_axis=0, concat_axis=0, tiled=True)]
  transfers between devices with their start and end apart: 7 -> 7, of which waited for: 6 -> 6; matrix products, arithmetic and copies ran while one was open for 25% -> 27% of each run, Pallas kernels for 0% -> 0%
where the time goes in v1:
time: 541 us; the launch traced here: 535 us
  waiting for transfers between devices  341 us (63%)
  local copies, waits for them, and re-layouts  65.5 us (12%)
  other arithmetic  60.5 us (11%)
  matrix products  31.6 us (6%)
  starting transfers between devices  22.4 us (4%)
  between operations  14.7 us (3%)
    all_to_all x1, waiting for transfers between devices, on_device(): lax.all_to_all(jnp.stack([saved_rows] * lax.axis_size('expert')), 'expert...  155 us
    all_gather x1, waiting for transfers between devices, on_device(): gathered = lax.all_gather(rows_fwd, 'expert', axis=0, tiled=True)  113 us
    all_to_all x1, waiting for transfers between devices, on_device(): lax.all_to_all(back_rows, 'expert', split_axis=0, concat_axis=0, tiled=True)  31.3 us
    all_gather x1, waiting for transfers between devices, on_device(): lax.all_gather(grads_in, 'expert', axis=0, tiled=True)  28.4 us
    unnamed x8, other arithmetic  15.7 us
    ppermute x2, waiting for transfers between devices, passed_along(): lax.ppermute(value, axis, [(i, (i + by) % devices) for i in range(devices)])  13.1 us
    gather x1, local copies, waits for them, and re-layouts, on_device(): grads_all[picked_back]  11.6 us
    gather x1, local copies, waits for them, and re-layouts, on_device(): gathered[picked]  11.5 us
  transfers between devices with their start and end apart: 7, of which 6 were waited for; matrix products, arithmetic and copies ran while one was open for 27% of the time, Pallas kernels for 0%

profile of v1, /device:TPU:4, one launch (start us, length us, event | category | flops | bytes accessed | tf_op | source)
XLA Modules:
  0.0 535.3 jit_solution(5695746399818909318)
XLA Ops:
  7.3 6.3 %collective-permute-done.1 = bf16[64,3584]{1,0:T(8,128)(2,1)S(1)} collective-permute-done((bf16[64,3584]{1,0:T(8,128)(2,1)}, bf16[64,3584]{1,0:T(8,128)(2,1)S(1)}, u32[]{:S(2)}, u32[]{:S(2)}) %collective-permute-start.1) | collective-permute-done | bytes 458784 | tf_op jit(solution)/shard_map/ppermute | solution.py:12
  13.6 0.8 copy-done.1
  14.4 4.7 stack.8
  19.1 11.4 %all-to-all-start.1 = ((bf16[16,64,3584]{2,1,0:T(8,128)(2,1)}), bf16[16,64,3584]{2,1,0:T(8,128)(2,1)}, u32[]{:S(2)}, u32[]{:S(2)}) async-start(bf16[16,64,3584]{2,1,0:T(8,128)(2,1)} %stack.8), calls=%async_computation.1 | async-start | bytes 14680064 | tf_op jit(solution)/shard_map/all_to_all | solution.py:106
  30.6 1.4 collective-permute-start
  32.0 6.8 %collective-permute-done = bf16[64,3584]{1,0:T(8,128)(2,1)S(1)} collective-permute-done((bf16[64,3584]{1,0:T(8,128)(2,1)}, bf16[64,3584]{1,0:T(8,128)(2,1)S(1)}, u32[]{:S(2)}, u32[]{:S(2)}) %collective-permute-start) | collective-permute-done | bytes 458784 | tf_op jit(solution)/shard_map/ppermute | solution.py:12
  38.8 0.8 copy-done.3
  39.6 0.6 broadcast.1194
  40.2 0.7 fusion.108
  40.9 0.3 copy.52
  41.3 0.9 compare_select_fusion.1
  42.2 1.3 copy.53
  43.5 0.3 copy.61
  43.8 0.9 compare_select_fusion
  44.7 1.3 copy.62
  46.5 7.4 %scatter_custom_fusion.10 = s32[320]{0:T(512)S(1)} fusion(s32[1024]{0:T(1024)S(1)} %reshape.1358, s32[1024]{0:T(1024)S(1)} %broadcast.1073, s32[]{:T(128)} %constant.206.clone.1), kind=kCustom, calls=%fused_computation.151 | custom fusion | flops 1024 | bytes 1284
  54.7 8.1 %scatter_custom_fusion.11 = s32[320]{0:T(512)S(1)} fusion(s32[1024]{0:T(1024)S(1)} %reshape.1364, s32[1024]{0:T(1024)S(1)} %broadcast.1073, s32[]{:T(128)} %constant.206.clone.1), kind=kCustom, calls=%fused_computation.149 | custom fusion | flops 1024 | bytes 1284
  64.2 2.5 gather_fusion.3
  66.7 154.9 %all-to-all-done.1 = bf16[16,64,3584]{2,1,0:T(8,128)(2,1)} async-done(((bf16[16,64,3584]{2,1,0:T(8,128)(2,1)}), bf16[16,64,3584]{2,1,0:T(8,128)(2,1)}, u32[]{:S(2)}, u32[]{:S(2)}) %all-to-all-start.1) | async-done | bytes 7340064 | tf_op jit(solution)/shard_map/all_to_all | solution.py:106
  221.6 11.5 %gather_fusion.4 = bf16[320,3584]{1,0:T(8,128)(2,1)} fusion(bf16[1024,3584]{1,0:T(8,128)(2,1)} %bitcast.26, s32[1024]{0:T(1024)S(1)} %pad_clamp_fusion), kind=kCustom, calls=%fused_computation.4 | custom fusion | bytes 4588800 | tf_op jit(solution)/shard_map/gather | solution.py:114
  233.1 3.8 fusion.12
  236.9 28.4 %all-gather.5.cloned.1.call-done = bf16[1024,3584]{1,0:T(8,128)(2,1)} async-done(((bf16[64,3584]{1,0:T(8,128)(2,1)}), bf16[1024,3584]{1,0:T(8,128)(2,1)}) %all-gather.5.cloned.1.call-update) | async-done | bytes 7340048 | tf_op jit(solution)/shard_map/all_gather | solution.py:109
  265.3 11.6 %gather_fusion.2 = bf16[320,3584]{1,0:T(8,128)(2,1)} fusion(bf16[1024,3584]{1,0:T(8,128)(2,1)} %all-gather.5.cloned.1.call-done, s32[1024]{0:T(1024)S(1)} %pad_clamp_fusion), kind=kCustom, calls=%fused_computation.2 | custom fusion | bytes 4588800 | tf_op jit(solution)/shard_map/gather | solution.py:114
  276.9 4.7 fusion.25
  281.6 7.5 %fusion.10 = f32[320,3584]{1,0:T(8,128)} fusion(bf16[1,3584,384]{2,1,0:T(8,128)(2,1)} %param.17, f32[320,384]{1,0:T(8,128)} %fusion.25, bf16[320,3584]{1,0:T(8,128)(2,1)} %gather_fusion.4, bf16[1,3584,384]{2,1,0:T(8,128)(2,1)S(1)} %copy-done, f32[320,384]{1,0:T(8,128)S(1)} %fusion.12), kind=kOutput, calls=%fused_computation.31 | convolution fusion | flops 1762836480 | bytes 13369344 | tf_op jit(solution)/shard_map/dot_general | solution.py:40
  289.1 5.3 fusion.1
  294.4 4.1 reshape.1214
  298.5 4.6 all-to-all-start.2
  303.3 2.5 gather_fusion.1
  305.8 112.9 %all-gather.3.cloned.1.call-done = bf16[1024,3584]{1,0:T(8,128)(2,1)} async-done(((bf16[64,3584]{1,0:T(8,128)(2,1)}), bf16[1024,3584]{1,0:T(8,128)(2,1)}) %all-gather.3.cloned.1.call-update) | async-done | bytes 7340048 | tf_op jit(solution)/shard_map/all_gather | solution.py:97
  418.7 11.5 %gather_fusion = bf16[320,3584]{1,0:T(8,128)(2,1)} fusion(bf16[1024,3584]{1,0:T(8,128)(2,1)} %all-gather.3.cloned.1.call-done, s32[1024]{0:T(1024)S(1)} %pad_clamp_fusion.1), kind=kCustom, calls=%fused_computation | custom fusion | bytes 4588800 | tf_op jit(solution)/shard_map/gather | solution.py:100
  430.2 3.0 fusion.8
  433.2 7.4 %fusion = bf16[320,3584]{1,0:T(8,128)(2,1)} fusion(bf16[1,384,3584]{2,1,0:T(8,128)(2,1)} %param.19, f32[320]{0:T(512)S(1)} %convert_select_fusion.1, f32[320,384]{1,0:T(8,128)S(1)} %fusion.8, bf16[320,3584]{1,0:T(8,128)(2,1)} %gather_fusion, bf16[1,3584,384]{2,1,0:T(8,128)(2,1)} %param.17), kind=kOutput, calls=%fused_computation.21 | convolution fusion | flops 1764638720 | bytes 10585344 | tf_op jit(solution)/shard_map/dot_general | solution.py:26
  440.5 4.1 reshape.1206
  444.7 4.8 all-to-all-start
  449.8 1.0 scatter_custom_fusion.7
  451.3 1.0 scatter_custom_fusion.8
  452.8 1.0 scatter_custom_fusion.6
  454.3 1.0 scatter_custom_fusion.5
  455.3 0.2 select_n.472
  455.5 0.7 fusion.82
  456.2 1.3 compare_select_fusion.34
  457.5 1.2 compare_select_fusion.36
  459.2 1.0 scatter_custom_fusion.2
  460.2 0.2 select_n.457
  460.7 1.0 scatter_custom_fusion.3
  461.7 0.2 select_n.461
  462.2 1.0 scatter_custom_fusion.1
  463.2 0.2 select_n.453
  463.7 1.0 scatter_custom_fusion
  464.9 0.7 fusion.74
  465.6 1.3 compare_select_fusion.38
  466.9 1.2 compare_select_fusion.40
  468.2 1.0 convert_element_type.258
  469.2 2.0 convert_element_type.235
  471.2 3.5 convert_reduce_fusion
  474.8 2.5 reshape.1354
  477.2 4.9 scatter_fusion.1
  482.1 2.0 convert_bitcast_fusion
  484.1 31.3 %all-to-all-done = bf16[16,20,3584]{2,1,0:T(8,128)(2,1)} async-done(((bf16[16,20,3584]{2,1,0:T(8,128)(2,1)}), bf16[16,20,3584]{2,1,0:T(8,128)(2,1)}, u32[]{:S(2)}, u32[]{:S(2)}) %all-to-all-start) | async-done | bytes 2293792 | tf_op jit(solution)/shard_map/all_to_all | solution.py:102
  515.4 3.5 convert_reduce_fusion.1
  518.8 2.5 reshape.1314
  521.3 4.9 scatter_fusion
  526.2 2.0 convert_bitcast_fusion.1
  (105 shorter events, 6.6 us)
Async XLA Ops:
  7.2 274.5 %copy-start = (bf16[1,3584,384]{2,1,0:T(8,128)(2,1)S(1)}, bf16[1,3584,384]{2,1,0:T(8,128)(2,1)}, u32[]{:S(2)}) copy-start(bf16[1,3584,384]{2,1,0:T(8,128)(2,1)} %param.18) | copy-start | bytes 8257540
  7.2 258.1 %all-gather.5.cloned.1.call-start = ((), (), s32[]{:S(2)}) async-start(), calls=%async_computation.4 | async-start | bytes 7798784 | tf_op jit(solution)/shard_map/all_gather | solution.py:109
  7.2 6.4 %collective-permute-start.1 = (bf16[64,3584]{1,0:T(8,128)(2,1)}, bf16[64,3584]{1,0:T(8,128)(2,1)S(1)}, u32[]{:S(2)}, u32[]{:S(2)}) collective-permute-start(bf16[64,3584]{1,0:T(8,128)(2,1)} %bitcast.89), channel_id=1, source_target_pairs={{0,240},{16,0},{32,16},{48,32},{64,48},{80,64},{96,80},{112,96},{1... | collective-permute-start | bytes 1376264 | tf_op jit(solution)/shard_map/ppermute | solution.py:12
  13.6 0.8 copy-start.1
  19.1 21.1 %copy-start.4 = (s32[1,1024]{1,0:T(1,128)S(1)}, s32[1,1024]{1,0:T(1,128)}, u32[]{:S(2)}) copy-start(s32[1,1024]{1,0:T(1,128)} %param.15) | copy-start | bytes 12292
  19.1 21.1 %copy-start.5 = (s32[1,1024]{1,0:T(1,128)S(1)}, s32[1,1024]{1,0:T(1,128)}, u32[]{:S(2)}) copy-start(s32[1,1024]{1,0:T(1,128)} %param.11) | copy-start | bytes 12292
  19.1 202.5 %all-to-all-start.1 = ((bf16[16,64,3584]{2,1,0:T(8,128)(2,1)}), bf16[16,64,3584]{2,1,0:T(8,128)(2,1)}, u32[]{:S(2)}, u32[]{:S(2)}) async-start(bf16[16,64,3584]{2,1,0:T(8,128)(2,1)} %stack.8), calls=%async_computation.1 | async-start | bytes 14680064 | tf_op jit(solution)/shard_map/all_to_all | solution.py:106
  30.5 15.5 %copy-start.9 = (s32[2]{0:T(128)S(1)}, s32[2]{0:T(128)}, u32[]{:S(2)}) copy-start(s32[2]{0:T(128)} %constant.228) | copy-start | bytes 28
  30.5 15.7 %copy-start.8 = (s32[2]{0:T(128)S(1)}, s32[2]{0:T(128)}, u32[]{:S(2)}) copy-start(s32[2]{0:T(128)} %constant.231) | copy-start | bytes 28
  30.5 33.6 %copy-start.6 = (bf16[1,1024]{1,0:T(2,128)(2,1)S(1)}, bf16[1,1024]{1,0:T(2,128)(2,1)}, u32[]{:S(2)}) copy-start(bf16[1,1024]{1,0:T(2,128)(2,1)} %param.16) | copy-start | bytes 6148
  30.5 388.2 %all-gather.3.cloned.1.call-start = ((), (), s32[]{:S(2)}) async-start(), calls=%async_computation.3 | async-start | bytes 7798784 | tf_op jit(solution)/shard_map/all_gather | solution.py:97
  30.6 8.2 %collective-permute-start = (bf16[64,3584]{1,0:T(8,128)(2,1)}, bf16[64,3584]{1,0:T(8,128)(2,1)S(1)}, u32[]{:S(2)}, u32[]{:S(2)}) collective-permute-start(bf16[64,3584]{1,0:T(8,128)(2,1)} %bitcast.90), channel_id=1, source_target_pairs={{0,16},{16,32},{32,48},{48,64},{64,80},{80,96},{96,112},{112,128},... | collective-permute-start | bytes 1376264 | tf_op jit(solution)/shard_map/ppermute | solution.py:12
  38.8 0.8 copy-start.3
  298.5 4.6 copy-start.7
  298.5 146.1 %all-to-all-start.2 = ((bf16[16,20,3584]{2,1,0:T(8,128)(2,1)}), bf16[16,20,3584]{2,1,0:T(8,128)(2,1)}, u32[]{:S(2)}, u32[]{:S(2)}) async-start(bf16[16,20,3584]{2,1,0:T(8,128)(2,1)} %reshape.1214), calls=%async_computation.2 | async-start | bytes 5505024 | tf_op jit(solution)/shard_map/all_to_all | solution.py:117
  444.7 23.6 %copy-start.2 = (bf16[64,3584]{1,0:T(8,128)(2,1)S(1)}, bf16[64,3584]{1,0:T(8,128)(2,1)}, u32[]{:S(2)}) copy-start(bf16[64,3584]{1,0:T(8,128)(2,1)} %copy-done.1) | copy-start | bytes 1376260
  444.7 70.7 %all-to-all-start = ((bf16[16,20,3584]{2,1,0:T(8,128)(2,1)}), bf16[16,20,3584]{2,1,0:T(8,128)(2,1)}, u32[]{:S(2)}, u32[]{:S(2)}) async-start(bf16[16,20,3584]{2,1,0:T(8,128)(2,1)} %reshape.1206), calls=%async_computation | async-start | bytes 5505024 | tf_op jit(solution)/shard_map/all_to_all | solution.py:102
Sparse Core Ops, SparseCore 0:
  14.5 250.7 all-gather.4
  268.4 150.2 all-gather.2
